TPU v7x, 768 devices: a whole 4x8x12 slice. The times are simulated.
768 devices in a mesh: dp: 8 (over y_hi, core), mp: 96 (over y_lo, z, x).
Axes of the slice: x: 4, y: 8 (y_hi: 4, y_lo: 2; y = y_hi * 2 + y_lo), z: 12, core: 2. Of those that a mesh axis runs over, the one named last changes fastest.
Arguments:
- inputs: bfloat16 [1024, 6144], P('dp', 'mp'), may hold values from -6 to 6
- out_grad: bfloat16 [1024, 6144], P('dp', 'mp'), may hold values from -6 to 6
- first_weight: bfloat16 [6144, 12288], P('dp', 'mp'), may hold values from -0.25 to 0.25
- second_weight: bfloat16 [12288, 6144], P('mp', 'dp'), may hold values from -0.078125 to 0.078125
Outputs:
- input_grad: bfloat16 [1024, 6144], P('dp', 'mp')
- weight_grad: bfloat16 [6144, 12288], P('dp', 'mp')
All inputs are finite; a program needn't handle non-finite values.
Results may differ from a plain program's by a relative error of at most 0.017.
Values may be sent and summed in bfloat16 or wider, within the bound.
A program may use at most 32 MiB of HBM per device.

v0:
```python
import math

import jax
import jax.numpy as jnp
from jax import lax
from jax.sharding import PartitionSpec as P


def activation(values):
    return jax.nn.gelu(values, approximate=False)


def contract_last(left, right):
    return lax.dot_general(
        left, right, (((1,), (1,)), ((), ())), preferred_element_type=jnp.float32
    )


def body(inputs, out_grad, first_weight, second_weight):
    tok_rows = inputs.shape[0]
    inputs_full, grad_full = (
        lax.all_gather(inputs, "mp", axis=1, tiled=True),
        lax.all_gather(out_grad, "mp", axis=1, tiled=True),
    )
    columns = grad_full
    back = contract_last(columns, lax.all_gather(second_weight, "dp", axis=1, tiled=True))
    first_full = lax.all_gather(first_weight, "dp", axis=0, tiled=True)
    hidden = jnp.dot(inputs_full, first_full, preferred_element_type=jnp.float32)
    _, pull = jax.vjp(activation, hidden)
    act_grad = pull(back)[0].astype(jnp.bfloat16)
    scale = 1.0 / math.sqrt(tok_rows * lax.axis_size("dp"))
    columns = inputs_full
    product = lax.dot_general(
        columns, act_grad, (((0,), (0,)), ((), ())), preferred_element_type=jnp.float32
    )
    weight_part = lax.psum_scatter(
        (product * scale).astype(jnp.bfloat16), "dp", scatter_dimension=0, tiled=True
    )
    input_part = lax.psum_scatter(
        contract_last(first_full, act_grad), "mp", scatter_dimension=0, tiled=True
    )
    input_grad = input_part.T.astype(jnp.bfloat16)
    return (input_grad, weight_part)


def solution(mesh):
    return jax.shard_map(
        body,
        mesh=mesh,
        in_specs=(P("dp", "mp"), P("dp", "mp"), P("dp", "mp"), P("mp", "dp")),
        out_specs=(P("dp", "mp"), P("dp", "mp")),
        check_vma=False,
    )
```

profile of v0, /device:TPU:16, one launch (start us, length us, event | category | flops | bytes accessed | tf_op | source)
XLA Modules:
  0.0 1521.7 jit_solution(390695317991053847)
XLA Ops:
  7.2 0.0 all-gather.11.cloned.1.call-start
  7.2 0.7 all-gather.11.cloned.1.call-update
  7.9 0.0 all-gather.9.cloned.1.call-start
  7.9 0.7 all-gather.9.cloned.1.call-update
  8.6 0.0 all-gather.7.cloned.1.call-start
  8.7 0.7 all-gather.7.cloned.1.call-update
  9.4 0.0 all-gather.5.cloned.1.call-start
  9.4 0.5 all-gather.5.cloned.1.call-update
  10.0 0.0 reduce-scatter.5.cloned.1.call-start
  10.0 44.4 %all-gather.11.cloned.1.call-done = bf16[128,6144]{1,0:T(8,128)(2,1)} async-done(((bf16[128,768]{1,0:T(8,128)(2,1)}), bf16[128,6144]{1,0:T(8,128)(2,1)}) %all-gather.11.cloned.1.call-update) | async-done | bytes 1572880 | tf_op jit(solution)/shard_map/all_gather | solution.py:26
  54.4 452.6 %all-gather.9.cloned.1.call-done = bf16[128,6144]{0,1:T(8,128)(2,1)} async-done(((bf16[128,64]{0,1:T(8,128)(2,1)}), bf16[128,6144]{0,1:T(8,128)(2,1)}) %all-gather.9.cloned.1.call-update) | async-done | bytes 1572880 | tf_op jit(solution)/shard_map/all_gather | solution.py:23
  507.1 2.5 fusion.141
  509.6 28.0 %all-gather.7.cloned.1.call-done = bf16[6144,128]{1,0:T(8,128)(2,1)} async-done(((bf16[768,128]{1,0:T(8,128)(2,1)}), bf16[6144,128]{1,0:T(8,128)(2,1)}) %all-gather.7.cloned.1.call-update) | async-done | bytes 1572880 | tf_op jit(solution)/shard_map/all_gather | solution.py:27
  537.6 452.5 %all-gather.5.cloned.1.call-done = bf16[128,6144]{0,1:T(8,128)(2,1)} async-done(((bf16[128,64]{0,1:T(8,128)(2,1)}), bf16[128,6144]{0,1:T(8,128)(2,1)}) %all-gather.5.cloned.1.call-update) | async-done | bytes 1572880 | tf_op jit(solution)/shard_map/all_gather | solution.py:22
  990.1 2.6 fusion.140
  992.7 1.9 fusion.1
  994.6 0.0 reduce-scatter.7.cloned.1.call-start
  994.7 2.1 convolution_bitcast_fusion
  996.8 2.3 copy.10
  999.1 29.5 %reduce-scatter.5.cloned.1.call-done = bf16[768,128]{0,1:T(8,128)(2,1)} async-done(((bf16[6144,128]{0,1:T(8,128)(2,1)}), bf16[768,128]{0,1:T(8,128)(2,1)}) %reduce-scatter.5.cloned.1.call-update) | async-done | bytes 196624 | tf_op jit(solution)/shard_map/reduce_scatter | solution.py:36
  1028.6 1.7 copy.9
  1030.3 483.0 %reduce-scatter.7.cloned.1.call-done = f32[64,128]{1,0:T(8,128)} async-done(((f32[6144,128]{1,0:T(8,128)}), f32[64,128]{1,0:T(8,128)}) %reduce-scatter.7.cloned.1.call-update) | async-done | bytes 32784
  1513.3 0.9 copy.11
  1514.2 0.7 copy.8
  (4 shorter events, 0.0 us)
Async XLA Ops:
  7.2 47.3 %all-gather.11.cloned.1.call-start = ((), (), s32[]{:S(2)}) async-start(), calls=%async_computation.5 | async-start | bytes 1769472 | tf_op jit(solution)/shard_map/all_gather | solution.py:26
  7.9 499.2 %all-gather.9.cloned.1.call-start = ((), (), s32[]{:S(2)}) async-start(), calls=%async_computation.4 | async-start | bytes 1589248 | tf_op jit(solution)/shard_map/all_gather | solution.py:23
  8.6 528.9 %all-gather.7.cloned.1.call-start = ((), (), s32[]{:S(2)}) async-start(), calls=%async_computation.3 | async-start | bytes 1769472 | tf_op jit(solution)/shard_map/all_gather | solution.py:27
  9.4 980.7 %all-gather.5.cloned.1.call-start = ((), (), s32[]{:S(2)}) async-start(), calls=%async_computation.2 | async-start | bytes 1589248 | tf_op jit(solution)/shard_map/all_gather | solution.py:22
  10.0 1018.6 %reduce-scatter.5.cloned.1.call-start = ((), (), s32[]{:S(2)}) async-start(), calls=%async_computation.6 | async-start | bytes 1769472 | tf_op jit(solution)/shard_map/reduce_scatter | solution.py:36
  990.1 2.6 copy-start
  994.6 518.7 %reduce-scatter.7.cloned.1.call-start = ((), (), s32[]{:S(2)}) async-start(), calls=%async_computation.7 | async-start | bytes 3178496
Sparse Core Ops, SparseCore 0:
  10.4 43.9 all-gather.10
  56.8 450.1 all-gather.8
  509.5 28.0 all-gather.6
  539.8 450.1 all-gather.4
  994.7 33.8 reduce-scatter.4
  1031.5 481.7 reduce-scatter.6
where the time goes:
time: 1520 us
  waiting for transfers between devices  1490 us (98%)
    unnamed x7, waiting for transfers between devices  486 us
    all_gather x1, waiting for transfers between devices, body(): lax.all_gather(out_grad, 'mp', axis=1, tiled=True)  453 us
    all_gather x1, waiting for transfers between devices, body(): lax.all_gather(inputs, 'mp', axis=1, tiled=True)  452 us
    all_gather x1, waiting for transfers between devices, body(): lax.all_gather(second_weight, 'dp', axis=1, tiled=True)  44.4 us
  transfers between devices with their start and end apart: 6, of which 6 were waited for; matrix products, arithmetic and copies ran while one was open for 1% of the time, Pallas kernels for 0%

commit v1 on v0

v1 whole, which is shorter than its diff:
```python
import functools
import math

import jax
import jax.numpy as jnp
from jax import lax
from jax.experimental import pallas as pl
from jax.experimental.pallas import tpu as pltpu
from jax.sharding import PartitionSpec as P

NX, NY, NC = 4, 8, 2
F32, BF16 = jnp.float32, jnp.bfloat16
ROOT_HALF, ROOT_TWO_PI = math.sqrt(0.5), math.sqrt(2.0 * math.pi)


def gelu_slope(v):
    cdf = 0.5 * (1.0 + lax.erf(v * ROOT_HALF))
    return cdf + v * jnp.exp(-0.5 * v * v) / ROOT_TWO_PI


def dot(a, b, ca, cb):
    return lax.dot_general(a, b, (((ca,), (cb,)), ((), ())), preferred_element_type=F32)


def kernel(nz, scale, xt, gt, w1, w2, ig_out, wg_out,
           buf, w1b, w2b, cs, cr, keep, ys, yr, actf, part, xin, far, zs, zr, fin, igr, wgs, wgr,
           loc, w_s, w_r, p1_s, p1_r, z_s, z_r, x_s, x_r, c_s, c_r, y_s, y_r, a_s, a_r, ac_s, ac_r,
           gx_s, gx_r, zz_s, zz_r, p2_s, p2_r, wg_s, wg_r):
    nj = nz // 2
    feat = xt.shape[0]
    depth = nj * feat
    tok = xt.shape[1]
    col = nz * NX
    dp, mp = lax.axis_index("dp"), lax.axis_index("mp")
    core, ylo = dp % 2, mp // col
    z, x = (mp % col) // NX, mp % NX
    y = (dp // 2) * 2 + ylo

    def at(x_, y_, z_, c_):
        return ((y_ // 2) * 2 + c_, (y_ % 2) * col + z_ * NX + x_)

    def send(src, dst, ssem, rsem, dev):
        return pltpu.make_async_remote_copy(
            src_ref=src, dst_ref=dst, send_sem=ssem, recv_sem=rsem,
            device_id=dev, device_id_type=pl.DeviceIdType.MESH)

    right, left = at((x + 1) % NX, y, z, core), at((x + 3) % NX, y, z, core)
    other = at(x, y, z, 1 - core)
    twin = at(x, y + 1 - 2 * ylo, z, core)
    ydev = [None] + [at(x, (y + d) % NY, z, core) for d in range(1, NY)]
    zdev = [None] + [at(x, y, (z + d) % nz, core) for d in range(1, nz)]
    plane, mine = mp // nj, mp % nj
    goal_z = (dp // NX) * nj + mine
    goal = (plane // 2, (plane % 2) * col + goal_z * NX + dp % NX)
    origin = ((z // nj) * NX + x, (dp * 2 + ylo) * nj + z % nj)
    stays = jnp.logical_and(goal[0] == dp, goal[1] == mp)

    half_rows = pl.ds(pl.multiple_of(ylo * depth, 128), depth)
    other_rows = pl.ds(pl.multiple_of((1 - ylo) * depth, 128), depth)
    lw1 = pltpu.make_async_copy(w1.at[half_rows, :], w1b.at[ylo], loc.at[0])
    lw2 = pltpu.make_async_copy(w2.at[:, half_rows], w2b.at[ylo], loc.at[1])
    lw1.start()
    lw2.start()

    barrier = pltpu.get_barrier_semaphore()

    def greet(dev):
        pl.semaphore_signal(barrier, inc=1, device_id=dev, device_id_type=pl.DeviceIdType.MESH)

    @pl.when(jnp.logical_not(stays))
    def _():
        greet(origin)
        greet(goal)
    for dev in [right, left, other] + ydev[1:] + zdev[1:]:
        greet(dev)
    peers = 3 + (NY - 1) + (nz - 1)

    @pl.when(stays)
    def _():
        pl.semaphore_wait(barrier, peers)

    @pl.when(jnp.logical_not(stays))
    def _():
        pl.semaphore_wait(barrier, peers + 2)

    pair = [(xt, 0), (gt, 1)]

    @pl.when(stays)
    def _():
        cps = [pltpu.make_async_copy(src, buf.at[0, goal_z, i], p1_r.at[i]) for src, i in pair]
        for cp in cps:
            cp.start()
        for cp in cps:
            cp.wait()

    @pl.when(jnp.logical_not(stays))
    def _():
        cps = [send(src, buf.at[0, goal_z, i], p1_s.at[i], p1_r.at[i], goal) for src, i in pair]
        for cp in cps:
            cp.start()
        for cp in cps:
            cp.wait()

    zcp = []
    for d in range(1, nz):
        cp = send(buf.at[0, z], buf.at[0, z], z_s.at[d - 1], z_r.at[z], zdev[d])
        cp.start()
        zcp.append(cp)
    wcp = [send(w1.at[other_rows, :], w1b.at[ylo], w_s.at[0], w_r.at[0], twin),
           send(w2.at[:, other_rows], w2b.at[ylo], w_s.at[1], w_r.at[1], twin)]
    for cp in wcp:
        cp.start()
    lw1.wait()
    lw2.wait()

    parts = [pl.ds(0, nj), pl.ds(nj, nj)]

    def xcp(way, i, rel, half):
        to = (rel + (3 if way == 0 else 1)) % NX
        return send(buf.at[rel, parts[half]], buf.at[to, parts[half]], x_s.at[way, i], x_r.at[way, i],
                    right if way == 0 else left)

    ways = [[xcp(0, 0, 0, 0), xcp(0, 1, 0, 1), xcp(0, 2, 3, 0)],
            [xcp(1, 1, 0, 0), xcp(1, 0, 0, 1), xcp(1, 2, 1, 1)]]
    for half in range(2):
        for t in range(half * nj, half * nj + nj):
            @pl.when(t != z)
            def _(t=t):
                send(buf.at[0, t], buf.at[0, t], z_s.at[0], z_r.at[t], right).wait_recv()
        ways[0][half].start()
        ways[1][half].start()
    for cp in wcp:
        cp.wait()

    def tokens(rel, which):
        pieces = [buf[rel, i * nj:(i + 1) * nj, which].reshape(depth, tok) for i in range(2)]
        return jnp.concatenate(pieces, axis=1)

    ccp = [send(cs.at[r], cr.at[r], c_s.at[r], c_r.at[r], other) for r in range(NX)]

    def project(r):
        xs, gs = tokens(r, 0), tokens(r, 1)
        cs[r, 0] = dot(w1b[1 - core], xs, 0, 0)
        cs[r, 1] = dot(w2b[1 - core], gs, 1, 0)
        ccp[r].start()
        keep[r, 0] = dot(w1b[core], xs, 0, 0)
        keep[r, 1] = dot(w2b[core], gs, 1, 0)

    ycp = {}
    rows = ys.shape[3]

    def spread(r):
        ccp[r].wait()
        for a in range(2):
            total = (keep[r, a] + cr[r, a]).astype(BF16)
            ys[r, :, a] = total.reshape(NY, rows, 2 * tok)
        for d in range(1, NY):
            cp = send(ys.at[r, (y + d) % NY], yr.at[r, d], y_s.at[r, d - 1], y_r.at[r, d - 1], ydev[d])
            cp.start()
            ycp[r, d] = cp

    project(0)
    ways[0][0].wait_recv()
    ways[0][2].start()
    ways[1][1].wait_recv()
    ways[1][2].start()
    spread(0)
    ways[0][1].wait_recv()
    project(3)
    ways[1][0].wait_recv()
    project(1)
    spread(3)
    spread(1)
    ways[0][2].wait_recv()
    ways[1][2].wait_recv()
    project(2)
    spread(2)

    order = [0, 3, 1, 2]
    acp = {}
    for r in order:
        hid = ys[r, y, 0].astype(F32)
        back = ys[r, y, 1].astype(F32)
        for d in range(1, NY):
            ycp[r, d].wait_recv()
            hid = hid + yr[r, d, 0].astype(F32)
            back = back + yr[r, d, 1].astype(F32)
        actf[r, core, y] = (back * gelu_slope(hid)).astype(BF16)
        for d in range(1, NY):
            cp = send(actf.at[r, core, y], actf.at[r, core, y], a_s.at[r, d - 1], a_r.at[r, d - 1], ydev[d])
            cp.start()
            acp[r, d] = cp
    accp = [send(actf.at[r, core], actf.at[r, core], ac_s.at[r], ac_r.at[r], other) for r in range(NX)]
    for r in order:
        for d in range(1, NY):
            acp[r, d].wait_recv()
        accp[r].start()

    gx = {
        1: send(part.at[1], xin.at[0], gx_s.at[0], gx_r.at[0], right),
        3: send(part.at[3], xin.at[1], gx_s.at[1], gx_r.at[1], left),
        "a": send(part.at[2, parts[0]], far.at[0], gx_s.at[2], gx_r.at[2], right),
        "b": send(part.at[2, parts[1]], far.at[1], gx_s.at[3], gx_r.at[3], left),
        "a2": send(far.at[0], far.at[2], gx_s.at[4], gx_r.at[4], right),
        "b2": send(far.at[1], far.at[3], gx_s.at[5], gx_r.at[5], left),
    }
    units = 2 * NY * rows

    def hidden_rows(r):
        return actf[r].reshape(units, 2 * tok)

    for r in [3, 1, 2, 0]:
        accp[r].wait()
        g = hidden_rows(r)
        half = units // 2
        value = dot(w1b[0], g[:half], 1, 0) + dot(w1b[1], g[half:], 1, 0)
        if r:
            for h in range(2):
                part[r, parts[h]] = value[:, h * tok:(h + 1) * tok].astype(BF16).reshape(nj, feat, tok)
            if r == 2:
                gx["a"].start()
                gx["b"].start()
            else:
                gx[r].start()
        else:
            own = value

    total = None
    for r in range(NX):
        term = dot(tokens(r, 0), hidden_rows(r)[:, :], 1, 1)
        total = term if total is None else total + term
    gx["a"].wait_recv()
    gx["a2"].start()
    gx["b"].wait_recv()
    gx["b2"].start()
    total = (total * scale).astype(BF16)
    width = wgs.shape[2]
    wgs[0] = total[:, :width]
    wgs[1] = total[:, width:]
    wcopy = send(wgs.at[1 - ylo], wgr, wg_s.at[0], wg_r.at[0], twin)
    wcopy.start()
    wg_out[half_rows, :] = wgs[ylo]

    gx[1].wait_recv()
    gx[3].wait_recv()
    gx["a2"].wait_recv()
    gx["b2"].wait_recv()
    for h in range(2):
        summed = own[:, h * tok:(h + 1) * tok].reshape(nj, feat, tok)
        summed = summed + xin[0, parts[h]].astype(F32) + xin[1, parts[h]].astype(F32) + far[2 + h].astype(F32)
        zs[parts[h]] = summed.astype(BF16)
    zz = []
    for d in range(1, nz):
        cp = send(zs.at[(z + d) % nz], zr.at[d], zz_s.at[d - 1], zz_r.at[d - 1], zdev[d])
        cp.start()
        zz.append(cp)
    result = zs[z].astype(F32)
    for d in range(1, nz):
        zz[d - 1].wait_recv()
        result = result + zr[d].astype(F32)
    fin[...] = result.astype(BF16)

    @pl.when(stays)
    def _():
        ig_out[...] = fin[...]

    @pl.when(jnp.logical_not(stays))
    def _():
        cp = send(fin, igr, p2_s.at[0], p2_r.at[0], origin)
        cp.start()
        cp.wait()
        ig_out[...] = igr[...]

    wcopy.wait()
    wg_out[other_rows, :] = wgr[...]
    for cp in zcp + zz + ways[0] + ways[1] + list(gx.values()) + list(ycp.values()) + list(acp.values()):
        cp.wait_send()


def body(inputs, out_grad, first_weight, second_weight):
    tok, feat = inputs.shape
    nz = lax.axis_size("mp") // (2 * NX)
    nj = nz // 2
    width = first_weight.shape[1]
    depth = nj * feat
    rows = width // NY
    scale = 1.0 / math.sqrt(tok * lax.axis_size("dp"))
    dma = pltpu.SemaphoreType.DMA
    vmem = pltpu.VMEM
    scratch = [
        vmem((NX, nz, 2, feat, tok), BF16),
        vmem((2, depth, width), BF16),
        vmem((2, width, depth), BF16),
        vmem((NX, 2, width, 2 * tok), F32),
        vmem((NX, 2, width, 2 * tok), F32),
        vmem((NX, 2, width, 2 * tok), F32),
        vmem((NX, NY, 2, rows, 2 * tok), BF16),
        vmem((NX, NY, 2, rows, 2 * tok), BF16),
        vmem((NX, NC, NY, rows, 2 * tok), BF16),
        vmem((NX, nz, feat, tok), BF16),
        vmem((2, nz, feat, tok), BF16),
        vmem((4, nj, feat, tok), BF16),
        vmem((nz, feat, tok), BF16),
        vmem((nz, feat, tok), BF16),
        vmem((feat, tok), BF16),
        vmem((feat, tok), BF16),
        vmem((2, depth, width), BF16),
        vmem((depth, width), BF16),
        dma((2,)), dma((2,)), dma((2,)), dma((2,)), dma((2,)),
        dma((nz - 1,)), dma((nz,)), dma((2, 3)), dma((2, 3)),
        dma((NX,)), dma((NX,)), dma((NX, NY - 1)), dma((NX, NY - 1)),
        dma((NX, NY - 1)), dma((NX, NY - 1)), dma((NX,)), dma((NX,)),
        dma((6,)), dma((6,)), dma((nz - 1,)), dma((nz - 1,)),
        dma((1,)), dma((1,)), dma((1,)), dma((1,)),
    ]
    ig, wg = pl.pallas_call(
        functools.partial(kernel, nz, scale),
        out_shape=(jax.ShapeDtypeStruct((feat, tok), BF16),
                   jax.ShapeDtypeStruct(first_weight.shape, BF16)),
        in_specs=[pl.BlockSpec(memory_space=pl.ANY)] * 4,
        out_specs=(pl.BlockSpec(memory_space=pltpu.VMEM),) * 2,
        scratch_shapes=scratch,
        compiler_params=pltpu.CompilerParams(
            collective_id=0, has_side_effects=True, vmem_limit_bytes=40 * 2 ** 20),
        name="block_backward",
    )(inputs.T, out_grad.T, first_weight, second_weight)
    return (ig.T, wg)


def solution(mesh):
    return jax.shard_map(
        body,
        mesh=mesh,
        in_specs=(P("dp", "mp"), P("dp", "mp"), P("dp", "mp"), P("mp", "dp")),
        out_specs=(P("dp", "mp"), P("dp", "mp")),
        check_vma=False,
    )
```

time: 1520 us -> 107 us (0.07)
  the two profiles are of different devices: /device:TPU:16 before, /device:TPU:49 now
where the time goes in v1:
time: 107 us
  Pallas kernels  102 us (95%)
  local copies, waits for them, and re-layouts  4.56 us (4%)
    pallas_call x1, Pallas kernels, body(): pl.pallas_call(functools.partial(kernel, nz, scale), out_shape=(jax.Shape...  102 us
    unnamed x10, local copies, waits for them, and re-layouts  4.56 us

profile of v1, /device:TPU:49, one launch (start us, length us, event | category | flops | bytes accessed | tf_op | source)
XLA Modules:
  0.0 107.1 jit_solution(5377161354197451368)
XLA Ops:
  0.6 0.0 copy-start
  0.6 0.9 copy-done
  1.6 0.0 copy-start.1
  1.6 0.9 copy-done.1
  2.5 0.0 copy-start.2
  2.5 0.7 copy-done.2
  3.2 0.0 copy-start.3
  3.2 0.7 copy-done.3
  3.9 101.9 %block_backward.1 = (bf16[64,128]{1,0:T(8,128)(2,1)S(1)}, bf16[768,128]{1,0:T(8,128)(2,1)S(1)}) custom-call(bf16[64,128]{1,0:T(8,128)(2,1)S(1)} %bitcast.4, bf16[64,128]{1,0:T(8,128)(2,1)S(1)} %bitcast.5, bf16[768,128]{1,0:T(8,128)(2,1)S(1)} %copy-done, bf16[128,768]{1,0:T(8,128)(2,1)S(1)} %copy-done.1), custom_call_target="tpu_custom_call" | custom-call | tf_op jit(solution)/shard_map/block_backward/pallas_call | solution.py:316
  105.8 0.6 copy.8
  106.5 0.7 copy.9
Async XLA Ops:
  0.6 0.9 copy-start
  1.6 0.9 copy-start.1
  2.5 0.7 copy-start.2
  3.2 0.7 copy-start.3

commit v2 on v0

v2 whole, which is shorter than its diff:
```python
import functools
import math

import jax
import jax.numpy as jnp
from jax import lax
from jax.experimental import pallas as pl
from jax.experimental.pallas import tpu as pltpu
from jax.sharding import PartitionSpec as P

NX, NY, NC = 4, 8, 2
F32, BF16 = jnp.float32, jnp.bfloat16
ROOT_HALF, ROOT_TWO_PI = math.sqrt(0.5), math.sqrt(2.0 * math.pi)


def gelu_slope(v):
    cdf = 0.5 * (1.0 + lax.erf(v * ROOT_HALF))
    return cdf + v * jnp.exp(-0.5 * v * v) / ROOT_TWO_PI


def dot(a, b, ca, cb):
    return lax.dot_general(a, b, (((ca,), (cb,)), ((), ())), preferred_element_type=F32)


def kernel(nz, scale, xt, gt, w1, w2, ig_out, wg_out,
           buf, w1b, w1t, w2b, cs, cr, keep, ys, yr, actf, part, xin, zs, zr, fin, igr, wgs, wgr,
           loc, w_s, w_r, p_s, p_r, x_s, x_r, c_s, c_r, y_s, y_r, a_s, a_r, ac_s, ac_r,
           gx_s, gx_r, zz_s, zz_r, p2_s, p2_r, wg_s, wg_r):
    nj = nz // 2
    feat, tok = xt.shape
    depth = nj * feat
    col = nz * NX
    rows = ys.shape[3]
    dp, mp = lax.axis_index("dp"), lax.axis_index("mp")
    core, ylo = dp % 2, mp // col
    z, x = (mp % col) // NX, mp % NX
    y = (dp // 2) * 2 + ylo
    pending = []

    def at(x_, y_, z_, c_):
        return ((y_ // 2) * 2 + c_, (y_ % 2) * col + z_ * NX + x_)

    def copy(src, dst, ssem, rsem, dev):
        return pltpu.make_async_remote_copy(
            src_ref=src, dst_ref=dst, send_sem=ssem, recv_sem=rsem,
            device_id=dev, device_id_type=pl.DeviceIdType.MESH)

    def send(*args):
        cp = copy(*args)
        cp.start()
        pending.append(cp)
        return cp

    xdev = [at((x + d) % NX, y, z, core) for d in range(NX)]
    other = at(x, y, z, 1 - core)
    twin = at(x, y + 1 - 2 * ylo, z, core)
    ydev = [at(x, (y + d) % NY, z, core) for d in range(NY)]
    zdev = [at(x, y, (z + d) % nz, core) for d in range(nz)]
    plane = mp // nj
    slot = (dp // NX) * nj + mp % nj
    goals = [(plane // 2, (plane % 2) * col + ((z + t) % nz) * NX + dp % NX) for t in range(nz)]
    here = jnp.logical_and(jnp.logical_and(plane // 2 == dp, plane % 2 == ylo), dp % NX == x)
    stays = jnp.logical_and(here, slot == z)

    def owner(s):
        return ((s // nj) * NX + x, (dp * 2 + ylo) * nj + s % nj)

    def unless(condition, action):
        pl.when(jnp.logical_not(condition))(action)

    half_rows = pl.ds(pl.multiple_of(ylo * depth, 128), depth)
    other_rows = pl.ds(pl.multiple_of((1 - ylo) * depth, 128), depth)
    lw1 = pltpu.make_async_copy(w1.at[half_rows, :], w1b.at[ylo], loc.at[0])
    lw2 = pltpu.make_async_copy(w2.at[:, half_rows], w2b.at[ylo], loc.at[1])
    lw1.start()
    lw2.start()

    barrier = pltpu.get_barrier_semaphore()

    def greet(dev):
        pl.semaphore_signal(barrier, inc=1, device_id=dev, device_id_type=pl.DeviceIdType.MESH)

    for s in range(nz):
        unless(jnp.logical_and(here, slot == s), functools.partial(greet, owner(s)))
    unless(stays, lambda: greet((goals[0][0], (plane % 2) * col + slot * NX + dp % NX)))
    for dev in xdev[1:] + [other] + ydev[1:] + zdev[1:]:
        greet(dev)
    peers = (NX - 1) + 1 + (NY - 1) + (nz - 1) + nz + 1
    pl.semaphore_wait(barrier, peers - jnp.where(here, 1, 0) - jnp.where(stays, 1, 0))
    sources = [xt, gt]
    spots = [nz // 2] + [d for i in range(1, nz // 2) for d in (nz // 2 - i, nz // 2 + i)]

    def p_copy(w, t):
        return copy(sources[w], buf.at[w, 0, slot], p_s.at[w, t], p_r.at[w, slot], goals[t])

    def p_local(w):
        return pltpu.make_async_copy(sources[w], buf.at[w, 0, slot], loc.at[2 + w])

    for w in range(2):
        for t in spots:
            cp = p_copy(w, t)
            cp.start()
            pending.append(cp)
        pl.when(here)(p_local(w).start)
        unless(here, p_copy(w, 0).start)
    wcp = [send(w1.at[other_rows, :], w1b.at[ylo], w_s.at[0], w_r.at[0], twin),
           send(w2.at[:, other_rows], w2b.at[ylo], w_s.at[1], w_r.at[1], twin)]
    for w in range(2):
        pl.when(here)(p_local(w).wait)
    halves = [pl.ds(0, nj), pl.ds(nj, nj)]

    def x_copy(w, h, d):
        return copy(buf.at[w, 0, halves[h]], buf.at[w, NX - d, halves[h]],
                    x_s.at[w, h, d - 1], x_r.at[w, h, d - 1], xdev[d])

    def along_x(w, h):
        for s in range(h * nj, h * nj + nj):
            unless(jnp.logical_and(here, slot == s),
                   copy(sources[w], buf.at[w, 0, s], p_s.at[w, 0], p_r.at[w, s], goals[0]).wait_recv)
        for d in (2, 1, 3):
            cp = x_copy(w, h, d)
            cp.start()
            pending.append(cp)

    def tokens(w, h):
        return jnp.concatenate(
            [buf[w, r, h * nj:(h + 1) * nj].reshape(depth, tok) for r in range(NX)], axis=1)

    weight = [w1t, w2b]

    def c_copy(w, h):
        return copy(cs.at[w, h], cr.at[w, h], c_s.at[w, h], c_r.at[w, h], other)

    def project(w, h):
        for d in (1, 3, 2):
            x_copy(w, h, d).wait_recv()
        t = tokens(w, h)
        cs[w, h] = dot(weight[w][1 - core], t, 1, 0)
        cp = c_copy(w, h)
        cp.start()
        pending.append(cp)
        keep[w, h] = dot(weight[w][core], t, 1, 0)

    def y_copy(w, h, d):
        return copy(ys.at[w, h, (y + d) % NY], yr.at[w, h, d], y_s.at[w, h, d - 1], y_r.at[w, h, d - 1], ydev[d])

    def spread(w, h):
        c_copy(w, h).wait_recv()
        ys[w, h] = (keep[w, h] + cr[w, h]).astype(BF16).reshape(NY, rows, NX * tok)
        for d in (4, 3, 5, 2, 6, 1, 7):
            cp = y_copy(w, h, d)
            cp.start()
            pending.append(cp)

    along_x(0, 0)
    along_x(0, 1)
    lw1.wait()
    wcp[0].wait_recv()
    for i in range(2):
        w1t[i] = w1b[i].T
    lw2.wait()
    wcp[1].wait_recv()
    along_x(1, 0)
    project(0, 0)
    along_x(1, 1)
    project(0, 1)
    spread(0, 0)
    project(1, 0)
    spread(0, 1)
    spread(1, 0)
    project(1, 1)
    spread(1, 1)

    def a_copy(h, d):
        return copy(actf.at[h, core, y], actf.at[h, core, y], a_s.at[h, d - 1], a_r.at[h, d - 1], ydev[d])

    def act(h):
        sums = []
        for w in range(2):
            total = ys[w, h, y].astype(F32)
            for d in range(1, NY):
                y_copy(w, h, d).wait_recv()
                total = total + yr[w, h, d].astype(F32)
            sums.append(total)
        actf[h, core, y] = (sums[1] * gelu_slope(sums[0])).astype(BF16)
        for d in (4, 3, 5, 2, 6, 1, 7):
            cp = a_copy(h, d)
            cp.start()
            pending.append(cp)

    def ac_copy(h):
        return copy(actf.at[h, core], actf.at[h, core], ac_s.at[h], ac_r.at[h], other)

    def to_other(h):
        for d in range(1, NY):
            a_copy(h, d).wait_recv()
        cp = ac_copy(h)
        cp.start()
        pending.append(cp)

    def hidden_rows(h):
        return actf[h].reshape(NC * NY * rows, NX * tok)

    def g_copy(h, r):
        return copy(part.at[r, halves[h]], xin.at[r, halves[h]], gx_s.at[h, r - 1], gx_r.at[h, r - 1], xdev[r])

    def back_to_features(h):
        ac_copy(h).wait_recv()
        g = hidden_rows(h)
        half = NY * rows
        value = dot(w1b[0], g[:half], 1, 0) + dot(w1b[1], g[half:], 1, 0)
        for r in (2, 1, 3):
            part[r, halves[h]] = value[:, r * tok:(r + 1) * tok].astype(BF16).reshape(nj, feat, tok)
            cp = g_copy(h, r)
            cp.start()
            pending.append(cp)
        return value[:, :tok]

    def zz_copy(d):
        return copy(zs.at[(z + d) % nz], zr.at[d], zz_s.at[d - 1], zz_r.at[d - 1], zdev[d])

    def along_z(h, own):
        summed = own.reshape(nj, feat, tok)
        for r in (1, 3, 2):
            g_copy(h, r).wait_recv()
            summed = summed + xin[r, halves[h]].astype(F32)
        zs[halves[h]] = summed.astype(BF16)
        for t in range(h * nj, h * nj + nj):
            d = (t - z + nz) % nz
            unless(t == z, copy(zs.at[t], zr.at[d], zz_s.at[d - 1], zz_r.at[d - 1],
                                (dp, ylo * col + t * NX + x)).start)

    act(0)
    act(1)
    to_other(0)
    own = [back_to_features(0)]
    to_other(1)
    own.append(back_to_features(1))
    along_z(0, own[0])

    total = (dot(tokens(0, 0), hidden_rows(0), 1, 1) + dot(tokens(0, 1), hidden_rows(1), 1, 1)) * scale
    width = wgs.shape[2]
    for i in range(2):
        wgs[i] = total[:, i * width:(i + 1) * width].astype(BF16)
    wcopy = send(wgs.at[1 - ylo], wgr, wg_s.at[0], wg_r.at[0], twin)
    wg_out[half_rows, :] = wgs[ylo]

    along_z(1, own[1])
    result = zs[z].astype(F32)
    for d in range(1, nz):
        zz_copy(d).wait_recv()
        result = result + zr[d].astype(F32)
    fin[...] = result.astype(BF16)

    @pl.when(stays)
    def _():
        ig_out[...] = fin[...]

    @pl.when(jnp.logical_not(stays))
    def _():
        cp = copy(fin, igr, p2_s.at[0], p2_r.at[0], owner(z))
        cp.start()
        cp.wait()
        ig_out[...] = igr[...]

    wcopy.wait_recv()
    wg_out[other_rows, :] = wgr[...]
    for w in range(2):
        unless(here, p_copy(w, 0).wait_send)
    for d in range(1, nz):
        zz_copy(d).wait_send()
    for cp in pending:
        cp.wait_send()


def body(inputs, out_grad, first_weight, second_weight):
    tok, feat = inputs.shape
    nz = lax.axis_size("mp") // (2 * NX)
    nj = nz // 2
    width = first_weight.shape[1]
    depth = nj * feat
    rows = width // NY
    scale = 1.0 / math.sqrt(tok * lax.axis_size("dp"))
    dma = pltpu.SemaphoreType.DMA
    vmem = pltpu.VMEM
    scratch = [
        vmem((2, NX, nz, feat, tok), BF16),
        vmem((2, depth, width), BF16),
        vmem((2, width, depth), BF16),
        vmem((2, width, depth), BF16),
        vmem((2, 2, width, NX * tok), F32),
        vmem((2, 2, width, NX * tok), F32),
        vmem((2, 2, width, NX * tok), F32),
        vmem((2, 2, NY, rows, NX * tok), BF16),
        vmem((2, 2, NY, rows, NX * tok), BF16),
        vmem((2, NC, NY, rows, NX * tok), BF16),
        vmem((NX, nz, feat, tok), BF16),
        vmem((NX, nz, feat, tok), BF16),
        vmem((nz, feat, tok), BF16),
        vmem((nz, feat, tok), BF16),
        vmem((feat, tok), BF16),
        vmem((feat, tok), BF16),
        vmem((2, depth, width), BF16),
        vmem((depth, width), BF16),
        dma((4,)), dma((2,)), dma((2,)), dma((2, nz)), dma((2, nz)),
        dma((2, 2, NX - 1)), dma((2, 2, NX - 1)), dma((2, 2)), dma((2, 2)),
        dma((2, 2, NY - 1)), dma((2, 2, NY - 1)), dma((2, NY - 1)), dma((2, NY - 1)),
        dma((2,)), dma((2,)), dma((2, NX - 1)), dma((2, NX - 1)), dma((nz - 1,)), dma((nz - 1,)),
        dma((1,)), dma((1,)), dma((1,)), dma((1,)),
    ]
    ig, wg = pl.pallas_call(
        functools.partial(kernel, nz, scale),
        out_shape=(jax.ShapeDtypeStruct((feat, tok), BF16),
                   jax.ShapeDtypeStruct(first_weight.shape, BF16)),
        in_specs=[pl.BlockSpec(memory_space=pl.ANY)] * 4,
        out_specs=(pl.BlockSpec(memory_space=pltpu.VMEM),) * 2,
        scratch_shapes=scratch,
        compiler_params=pltpu.CompilerParams(
            collective_id=0, has_side_effects=True, vmem_limit_bytes=62 * 2 ** 20),
        name="block_backward",
    )(inputs.T, out_grad.T, first_weight, second_weight)
    return (ig.T, wg)


def solution(mesh):
    return jax.shard_map(
        body,
        mesh=mesh,
        in_specs=(P("dp", "mp"), P("dp", "mp"), P("dp", "mp"), P("mp", "dp")),
        out_specs=(P("dp", "mp"), P("dp", "mp")),
        check_vma=False,
    )
```

time: 1520 us -> 98.8 us (0.07)
  the two profiles are of different devices: /device:TPU:16 before, /device:TPU:120 now
where the time goes in v2:
time: 98.8 us; the launch traced here: 98.5 us
  Pallas kernels  95 us (96%)
  local copies, waits for them, and re-layouts  2.94 us (3%)
    pallas_call x1, Pallas kernels, body(): pl.pallas_call(functools.partial(kernel, nz, scale), out_shape=(jax.Shape...  95 us
    unnamed x2, local copies, waits for them, and re-layouts  2.94 us

profile of v2, /device:TPU:120, one launch (start us, length us, event | category | flops | bytes accessed | tf_op | source)
XLA Modules:
  0.0 98.5 jit_solution(15602729602670255485)
XLA Ops:
  0.6 95.0 %block_backward.1 = (bf16[64,128]{1,0:T(8,128)(2,1)}, bf16[768,128]{1,0:T(8,128)(2,1)}) custom-call(bf16[64,128]{1,0:T(8,128)(2,1)} %bitcast.4, bf16[64,128]{1,0:T(8,128)(2,1)} %bitcast.5, bf16[768,128]{1,0:T(8,128)(2,1)} %w1.1, bf16[128,768]{1,0:T(8,128)(2,1)} %w2.1), custom_call_target="tpu_custom_call" | custom-call | tf_op jit(solution)/shard_map/block_backward/pallas_call | solution.py:311
  95.6 1.3 %copy.8 = bf16[128,64]{0,1:T(8,128)(2,1)} copy(bf16[128,64]{0,1:T(8,128)(2,1)} %bitcast.3) | data formatting | bytes 32768
  96.9 1.6 %copy.9 = bf16[768,128]{1,0:T(8,128)(2,1)} copy(bf16[768,128]{1,0:T(8,128)(2,1)} %get-tuple-element.9) | data formatting | bytes 393216

commit v3 on v2

--- a/solution.py
+++ b/solution.py
@@ -9,6 +9,9 @@
 from jax.sharding import PartitionSpec as P
 
 NX, NY, NC = 4, 8, 2
+ORDER = (0, 2, 1, 3)
+X_STEPS, Y_STEPS = (2, 1, 3), (4, 3, 5, 2, 6, 1, 7)
+CHUNKS = ((0, 0, 4), (1, 0, 4))
 F32, BF16 = jnp.float32, jnp.bfloat16
 ROOT_HALF, ROOT_TWO_PI = math.sqrt(0.5), math.sqrt(2.0 * math.pi)
 
@@ -23,7 +26,7 @@
 
 
 def kernel(nz, scale, xt, gt, w1, w2, ig_out, wg_out,
-           buf, w1b, w1t, w2b, cs, cr, keep, ys, yr, actf, part, xin, zs, zr, fin, igr, wgs, wgr,
+           buf, u, w1b, w1t, w2b, cs, cr, keep, ys, yr, actf, part, xin, zs, zr, fin, igr, wgs, wgr,
            loc, w_s, w_r, p_s, p_r, x_s, x_r, c_s, c_r, y_s, y_r, a_s, a_r, ac_s, ac_r,
            gx_s, gx_r, zz_s, zz_r, p2_s, p2_r, wg_s, wg_r):
     nj = nz // 2
@@ -58,7 +61,7 @@
     zdev = [at(x, y, (z + d) % nz, core) for d in range(nz)]
     plane = mp // nj
     slot = (dp // NX) * nj + mp % nj
-    goals = [(plane // 2, (plane % 2) * col + ((z + t) % nz) * NX + dp % NX) for t in range(nz)]
+    goals = [(plane // 2, (plane % 2) * col + t * NX + dp % NX) for t in range(nz)]
     here = jnp.logical_and(jnp.logical_and(plane // 2 == dp, plane % 2 == ylo), dp % NX == x)
     stays = jnp.logical_and(here, slot == z)
 
@@ -70,6 +73,9 @@
 
     half_rows = pl.ds(pl.multiple_of(ylo * depth, 128), depth)
     other_rows = pl.ds(pl.multiple_of((1 - ylo) * depth, 128), depth)
+    lu = [pltpu.make_async_copy(xt, u.at[0], loc.at[4]), pltpu.make_async_copy(gt, u.at[1], loc.at[5])]
+    for cp in lu:
+        cp.start()
     lw1 = pltpu.make_async_copy(w1.at[half_rows, :], w1b.at[ylo], loc.at[0])
     lw2 = pltpu.make_async_copy(w2.at[:, half_rows], w2b.at[ylo], loc.at[1])
     lw1.start()
@@ -87,8 +93,9 @@
         greet(dev)
     peers = (NX - 1) + 1 + (NY - 1) + (nz - 1) + nz + 1
     pl.semaphore_wait(barrier, peers - jnp.where(here, 1, 0) - jnp.where(stays, 1, 0))
-    sources = [xt, gt]
-    spots = [nz // 2] + [d for i in range(1, nz // 2) for d in (nz // 2 - i, nz // 2 + i)]
+    sources = [u.at[0], u.at[1]]
+    for cp in lu:
+        cp.wait()
 
     def p_copy(w, t):
         return copy(sources[w], buf.at[w, 0, slot], p_s.at[w, t], p_r.at[w, slot], goals[t])
@@ -97,12 +104,9 @@
         return pltpu.make_async_copy(sources[w], buf.at[w, 0, slot], loc.at[2 + w])
 
     for w in range(2):
-        for t in spots:
-            cp = p_copy(w, t)
-            cp.start()
-            pending.append(cp)
+        for t in range(nz):
+            unless(jnp.logical_and(here, z == t), p_copy(w, t).start)
         pl.when(here)(p_local(w).start)
-        unless(here, p_copy(w, 0).start)
     wcp = [send(w1.at[other_rows, :], w1b.at[ylo], w_s.at[0], w_r.at[0], twin),
            send(w2.at[:, other_rows], w2b.at[ylo], w_s.at[1], w_r.at[1], twin)]
     for w in range(2):
@@ -113,108 +117,134 @@
         return copy(buf.at[w, 0, halves[h]], buf.at[w, NX - d, halves[h]],
                     x_s.at[w, h, d - 1], x_r.at[w, h, d - 1], xdev[d])
 
+    def begin(cp):
+        cp.start()
+        pending.append(cp)
+
     def along_x(w, h):
         for s in range(h * nj, h * nj + nj):
             unless(jnp.logical_and(here, slot == s),
                    copy(sources[w], buf.at[w, 0, s], p_s.at[w, 0], p_r.at[w, s], goals[0]).wait_recv)
-        for d in (2, 1, 3):
-            cp = x_copy(w, h, d)
-            cp.start()
-            pending.append(cp)
-
-    def tokens(w, h):
+        for d in X_STEPS:
+            begin(x_copy(w, h, d))
+
+    def arrived(w, h, r):
+        if r:
+            x_copy(w, h, NX - r).wait_recv()
+
+    whole = [(0, 0, NX), (1, 0, NX)]
+    chunks = [whole, CHUNKS]
+
+    def lanes(chunk):
+        return pl.ds(chunk[1] * tok, (chunk[2] - chunk[1]) * tok)
+
+    def tokens(w, chunk):
+        h, lo, hi = chunk
         return jnp.concatenate(
-            [buf[w, r, h * nj:(h + 1) * nj].reshape(depth, tok) for r in range(NX)], axis=1)
+            [buf[w, ORDER[i], h * nj:(h + 1) * nj].reshape(depth, tok) for i in range(lo, hi)], axis=1)
 
     weight = [w1t, w2b]
 
-    def c_copy(w, h):
-        return copy(cs.at[w, h], cr.at[w, h], c_s.at[w, h], c_r.at[w, h], other)
-
-    def project(w, h):
-        for d in (1, 3, 2):
-            x_copy(w, h, d).wait_recv()
-        t = tokens(w, h)
-        cs[w, h] = dot(weight[w][1 - core], t, 1, 0)
-        cp = c_copy(w, h)
-        cp.start()
-        pending.append(cp)
-        keep[w, h] = dot(weight[w][core], t, 1, 0)
-
-    def y_copy(w, h, d):
-        return copy(ys.at[w, h, (y + d) % NY], yr.at[w, h, d], y_s.at[w, h, d - 1], y_r.at[w, h, d - 1], ydev[d])
-
-    def spread(w, h):
-        c_copy(w, h).wait_recv()
-        ys[w, h] = (keep[w, h] + cr[w, h]).astype(BF16).reshape(NY, rows, NX * tok)
-        for d in (4, 3, 5, 2, 6, 1, 7):
-            cp = y_copy(w, h, d)
-            cp.start()
-            pending.append(cp)
-
+    def c_copy(w, i):
+        h = chunks[w][i][0]
+        part_ = lanes(chunks[w][i])
+        return copy(cs.at[w, h, :, part_], cr.at[w, h, :, part_], c_s.at[w, i], c_r.at[w, i], other)
+
+    def project(w, i):
+        h, lo, hi = chunks[w][i]
+        for place in range(lo, hi):
+            arrived(w, h, ORDER[place])
+        t = tokens(w, chunks[w][i])
+        cs[w, h, :, lo * tok:hi * tok] = dot(weight[w][1 - core], t, 1, 0)
+        begin(c_copy(w, i))
+        keep[w, h, :, lo * tok:hi * tok] = dot(weight[w][core], t, 1, 0)
+
+    def y_copy(w, i, d):
+        h, part_ = chunks[w][i][0], lanes(chunks[w][i])
+        return copy(ys.at[w, h, (y + d) % NY, :, part_], yr.at[w, h, d, :, part_],
+                    y_s.at[w, i, d - 1], y_r.at[w, i, d - 1], ydev[d])
+
+    def spread(w, i):
+        h, lo, hi = chunks[w][i]
+        c_copy(w, i).wait_recv()
+        total = keep[w, h, :, lo * tok:hi * tok] + cr[w, h, :, lo * tok:hi * tok]
+        ys[w, h, :, :, lo * tok:hi * tok] = total.astype(BF16).reshape(NY, rows, (hi - lo) * tok)
+        for d in Y_STEPS:
+            begin(y_copy(w, i, d))
     along_x(0, 0)
     along_x(0, 1)
+    along_x(1, 0)
+    along_x(1, 1)
     lw1.wait()
     wcp[0].wait_recv()
     for i in range(2):
         w1t[i] = w1b[i].T
     lw2.wait()
     wcp[1].wait_recv()
-    along_x(1, 0)
     project(0, 0)
-    along_x(1, 1)
     project(0, 1)
     spread(0, 0)
+    spread(0, 1)
     project(1, 0)
-    spread(0, 1)
     spread(1, 0)
-    project(1, 1)
-    spread(1, 1)
-
-    def a_copy(h, d):
-        return copy(actf.at[h, core, y], actf.at[h, core, y], a_s.at[h, d - 1], a_r.at[h, d - 1], ydev[d])
-
-    def act(h):
+    for i in range(1, len(CHUNKS)):
+        project(1, i)
+    for i in range(1, len(CHUNKS)):
+        spread(1, i)
+
+    def a_copy(i, d):
+        h, part_ = CHUNKS[i][0], lanes(CHUNKS[i])
+        return copy(actf.at[h, core, y, :, part_], actf.at[h, core, y, :, part_],
+                    a_s.at[i, d - 1], a_r.at[i, d - 1], ydev[d])
+
+    def act(i):
+        h, lo, hi = CHUNKS[i]
         sums = []
         for w in range(2):
-            total = ys[w, h, y].astype(F32)
+            total = ys[w, h, y, :, lo * tok:hi * tok].astype(F32)
             for d in range(1, NY):
-                y_copy(w, h, d).wait_recv()
-                total = total + yr[w, h, d].astype(F32)
+                if w == 1:
+                    y_copy(w, i, d).wait_recv()
+                elif lo == 0:
+                    y_copy(w, h, d).wait_recv()
+                total = total + yr[w, h, d, :, lo * tok:hi * tok].astype(F32)
             sums.append(total)
-        actf[h, core, y] = (sums[1] * gelu_slope(sums[0])).astype(BF16)
-        for d in (4, 3, 5, 2, 6, 1, 7):
-            cp = a_copy(h, d)
-            cp.start()
-            pending.append(cp)
-
-    def ac_copy(h):
-        return copy(actf.at[h, core], actf.at[h, core], ac_s.at[h], ac_r.at[h], other)
-
-    def to_other(h):
+        actf[h, core, y, :, lo * tok:hi * tok] = (sums[1] * gelu_slope(sums[0])).astype(BF16)
+        for d in Y_STEPS:
+            begin(a_copy(i, d))
+
+    def ac_copy(i):
+        h, part_ = CHUNKS[i][0], lanes(CHUNKS[i])
+        return copy(actf.at[h, core, :, :, part_], actf.at[h, core, :, :, part_], ac_s.at[i], ac_r.at[i], other)
+
+    def to_other(i):
         for d in range(1, NY):
-            a_copy(h, d).wait_recv()
-        cp = ac_copy(h)
-        cp.start()
-        pending.append(cp)
-
-    def hidden_rows(h):
-        return actf[h].reshape(NC * NY * rows, NX * tok)
+            a_copy(i, d).wait_recv()
+        begin(ac_copy(i))
+
+    def hidden_rows(chunk):
+        h, lo, hi = chunk
+        return actf[h, :, :, :, lo * tok:hi * tok].reshape(NC * NY * rows, (hi - lo) * tok)
 
     def g_copy(h, r):
         return copy(part.at[r, halves[h]], xin.at[r, halves[h]], gx_s.at[h, r - 1], gx_r.at[h, r - 1], xdev[r])
 
-    def back_to_features(h):
-        ac_copy(h).wait_recv()
-        g = hidden_rows(h)
+    own = {}
+
+    def back_to_features(i):
+        h, lo, hi = CHUNKS[i]
+        ac_copy(i).wait_recv()
+        g = hidden_rows(CHUNKS[i])
         half = NY * rows
         value = dot(w1b[0], g[:half], 1, 0) + dot(w1b[1], g[half:], 1, 0)
-        for r in (2, 1, 3):
-            part[r, halves[h]] = value[:, r * tok:(r + 1) * tok].astype(BF16).reshape(nj, feat, tok)
-            cp = g_copy(h, r)
-            cp.start()
-            pending.append(cp)
-        return value[:, :tok]
+        for place in range(hi - 1, lo - 1, -1):
+            r = ORDER[place]
+            this = value[:, (place - lo) * tok:(place - lo + 1) * tok]
+            if r == 0:
+                own[h] = this
+            else:
+                part[r, halves[h]] = this.astype(BF16).reshape(nj, feat, tok)
+                begin(g_copy(h, r))
 
     def zz_copy(d):
         return copy(zs.at[(z + d) % nz], zr.at[d], zz_s.at[d - 1], zz_r.at[d - 1], zdev[d])
@@ -229,16 +259,16 @@
             d = (t - z + nz) % nz
             unless(t == z, copy(zs.at[t], zr.at[d], zz_s.at[d - 1], zz_r.at[d - 1],
                                 (dp, ylo * col + t * NX + x)).start)
-
-    act(0)
-    act(1)
+    for i in range(len(CHUNKS)):
+        act(i)
     to_other(0)
-    own = [back_to_features(0)]
-    to_other(1)
-    own.append(back_to_features(1))
+    back_to_features(0)
+    for i in range(1, len(CHUNKS)):
+        to_other(i)
+        back_to_features(i)
     along_z(0, own[0])
 
-    total = (dot(tokens(0, 0), hidden_rows(0), 1, 1) + dot(tokens(0, 1), hidden_rows(1), 1, 1)) * scale
+    total = sum(dot(tokens(0, c), hidden_rows(c), 1, 1) for c in whole) * scale
     width = wgs.shape[2]
     for i in range(2):
         wgs[i] = total[:, i * width:(i + 1) * width].astype(BF16)
@@ -266,7 +296,8 @@
     wcopy.wait_recv()
     wg_out[other_rows, :] = wgr[...]
     for w in range(2):
-        unless(here, p_copy(w, 0).wait_send)
+        for t in range(nz):
+            unless(jnp.logical_and(here, z == t), p_copy(w, t).wait_send)
     for d in range(1, nz):
         zz_copy(d).wait_send()
     for cp in pending:
@@ -285,6 +316,7 @@
     vmem = pltpu.VMEM
     scratch = [
         vmem((2, NX, nz, feat, tok), BF16),
+        vmem((2, feat, tok), BF16),
         vmem((2, depth, width), BF16),
         vmem((2, width, depth), BF16),
         vmem((2, width, depth), BF16),
@@ -302,10 +334,10 @@
         vmem((feat, tok), BF16),
         vmem((2, depth, width), BF16),
         vmem((depth, width), BF16),
-        dma((4,)), dma((2,)), dma((2,)), dma((2, nz)), dma((2, nz)),
-        dma((2, 2, NX - 1)), dma((2, 2, NX - 1)), dma((2, 2)), dma((2, 2)),
-        dma((2, 2, NY - 1)), dma((2, 2, NY - 1)), dma((2, NY - 1)), dma((2, NY - 1)),
-        dma((2,)), dma((2,)), dma((2, NX - 1)), dma((2, NX - 1)), dma((nz - 1,)), dma((nz - 1,)),
+        dma((6,)), dma((2,)), dma((2,)), dma((2, nz)), dma((2, nz)),
+        dma((2, 2, NX - 1)), dma((2, 2, NX - 1)), dma((2, 3)), dma((2, 3)),
+        dma((2, 3, NY - 1)), dma((2, 3, NY - 1)), dma((3, NY - 1)), dma((3, NY - 1)),
+        dma((3,)), dma((3,)), dma((2, NX - 1)), dma((2, NX - 1)), dma((nz - 1,)), dma((nz - 1,)),
         dma((1,)), dma((1,)), dma((1,)), dma((1,)),
     ]
     ig, wg = pl.pallas_call(

time: 98.8 us -> 97.3 us (0.985)
  the two profiles are of different devices: /device:TPU:120 before, /device:TPU:49 now
where the time goes in v3:
time: 97.3 us; the launch traced here: 97.1 us
  Pallas kernels  93.5 us (96%)
  local copies, waits for them, and re-layouts  2.94 us (3%)
    pallas_call x1, Pallas kernels, body(): pl.pallas_call(functools.partial(kernel, nz, scale), out_shape=(jax.Shape...  93.5 us
    unnamed x2, local copies, waits for them, and re-layouts  2.94 us

profile of v3, /device:TPU:49, one launch (start us, length us, event | category | flops | bytes accessed | tf_op | source)
XLA Modules:
  0.0 97.1 jit_solution(6666138157678245706)
XLA Ops:
  0.6 93.5 %block_backward.1 = (bf16[64,128]{1,0:T(8,128)(2,1)}, bf16[768,128]{1,0:T(8,128)(2,1)}) custom-call(bf16[64,128]{1,0:T(8,128)(2,1)} %bitcast.4, bf16[64,128]{1,0:T(8,128)(2,1)} %bitcast.5, bf16[768,128]{1,0:T(8,128)(2,1)} %w1.1, bf16[128,768]{1,0:T(8,128)(2,1)} %w2.1), custom_call_target="tpu_custom_call" | custom-call | tf_op jit(solution)/shard_map/block_backward/pallas_call | solution.py:343
  94.1 1.3 %copy.8 = bf16[128,64]{0,1:T(8,128)(2,1)} copy(bf16[128,64]{0,1:T(8,128)(2,1)} %bitcast.3) | data formatting | bytes 32768
  95.4 1.6 %copy.9 = bf16[768,128]{1,0:T(8,128)(2,1)} copy(bf16[768,128]{1,0:T(8,128)(2,1)} %get-tuple-element.9) | data formatting | bytes 393216

commit v4 on v3

--- a/solution.py
+++ b/solution.py
@@ -113,24 +113,29 @@
         pl.when(here)(p_local(w).wait)
     halves = [pl.ds(0, nj), pl.ds(nj, nj)]
 
-    def x_copy(w, h, d):
-        return copy(buf.at[w, 0, halves[h]], buf.at[w, NX - d, halves[h]],
-                    x_s.at[w, h, d - 1], x_r.at[w, h, d - 1], xdev[d])
+    runs = [[(h * nj, nj // 2), (h * nj + nj // 2, nj - nj // 2)] for h in range(2)]
+
+    def x_copy(w, h, k, d):
+        span = pl.ds(*runs[h][k])
+        return copy(buf.at[w, 0, span], buf.at[w, NX - d, span],
+                    x_s.at[w, h, k, d - 1], x_r.at[w, h, k, d - 1], xdev[d])
 
     def begin(cp):
         cp.start()
         pending.append(cp)
 
     def along_x(w, h):
-        for s in range(h * nj, h * nj + nj):
-            unless(jnp.logical_and(here, slot == s),
-                   copy(sources[w], buf.at[w, 0, s], p_s.at[w, 0], p_r.at[w, s], goals[0]).wait_recv)
-        for d in X_STEPS:
-            begin(x_copy(w, h, d))
+        for k, (first, count) in enumerate(runs[h]):
+            for s in range(first, first + count):
+                unless(jnp.logical_and(here, slot == s),
+                       copy(sources[w], buf.at[w, 0, s], p_s.at[w, 0], p_r.at[w, s], goals[0]).wait_recv)
+            for d in X_STEPS:
+                begin(x_copy(w, h, k, d))
 
     def arrived(w, h, r):
         if r:
-            x_copy(w, h, NX - r).wait_recv()
+            for k in range(2):
+                x_copy(w, h, k, NX - r).wait_recv()
 
     whole = [(0, 0, NX), (1, 0, NX)]
     chunks = [whole, CHUNKS]
@@ -335,7 +340,7 @@
         vmem((2, depth, width), BF16),
         vmem((depth, width), BF16),
         dma((6,)), dma((2,)), dma((2,)), dma((2, nz)), dma((2, nz)),
-        dma((2, 2, NX - 1)), dma((2, 2, NX - 1)), dma((2, 3)), dma((2, 3)),
+        dma((2, 2, 2, NX - 1)), dma((2, 2, 2, NX - 1)), dma((2, 3)), dma((2, 3)),
         dma((2, 3, NY - 1)), dma((2, 3, NY - 1)), dma((3, NY - 1)), dma((3, NY - 1)),
         dma((3,)), dma((3,)), dma((2, NX - 1)), dma((2, NX - 1)), dma((nz - 1,)), dma((nz - 1,)),
         dma((1,)), dma((1,)), dma((1,)), dma((1,)),

time: 97.3 us -> 97.7 us (level)
  no operation moved by 1% of the time
where the time goes in v4:
time: 97.7 us; the launch traced here: 97.5 us
  Pallas kernels  93.9 us (96%)
  local copies, waits for them, and re-layouts  2.94 us (3%)
    pallas_call x1, Pallas kernels, body(): pl.pallas_call(functools.partial(kernel, nz, scale), out_shape=(jax.Shape...  93.9 us
    unnamed x2, local copies, waits for them, and re-layouts  2.94 us

profile of v4, /device:TPU:49, one launch (start us, length us, event | category | flops | bytes accessed | tf_op | source)
XLA Modules:
  0.0 97.5 jit_solution(12075687183562912084)
XLA Ops:
  0.6 93.9 %block_backward.1 = (bf16[64,128]{1,0:T(8,128)(2,1)}, bf16[768,128]{1,0:T(8,128)(2,1)}) custom-call(bf16[64,128]{1,0:T(8,128)(2,1)} %bitcast.4, bf16[64,128]{1,0:T(8,128)(2,1)} %bitcast.5, bf16[768,128]{1,0:T(8,128)(2,1)} %w1.1, bf16[128,768]{1,0:T(8,128)(2,1)} %w2.1), custom_call_target="tpu_custom_call" | custom-call | tf_op jit(solution)/shard_map/block_backward/pallas_call | solution.py:348
  94.5 1.3 %copy.8 = bf16[128,64]{0,1:T(8,128)(2,1)} copy(bf16[128,64]{0,1:T(8,128)(2,1)} %bitcast.3) | data formatting | bytes 32768
  95.9 1.6 %copy.9 = bf16[768,128]{1,0:T(8,128)(2,1)} copy(bf16[768,128]{1,0:T(8,128)(2,1)} %get-tuple-element.9) | data formatting | bytes 393216

commit v5 on v3

--- a/solution.py
+++ b/solution.py
@@ -273,7 +273,9 @@
     for i in range(2):
         wgs[i] = total[:, i * width:(i + 1) * width].astype(BF16)
     wcopy = send(wgs.at[1 - ylo], wgr, wg_s.at[0], wg_r.at[0], twin)
-    wg_out[half_rows, :] = wgs[ylo]
+    stores = [pltpu.make_async_copy(wgs.at[ylo], wg_out.at[half_rows, :], loc.at[0]),
+              pltpu.make_async_copy(wgr, wg_out.at[other_rows, :], loc.at[1])]
+    stores[0].start()
 
     along_z(1, own[1])
     result = zs[z].astype(F32)
@@ -281,6 +283,12 @@
         zz_copy(d).wait_recv()
         result = result + zr[d].astype(F32)
     fin[...] = result.astype(BF16)
+    home = copy(fin, igr, p2_s.at[0], p2_r.at[0], owner(z))
+    unless(stays, home.start)
+    wcopy.wait_recv()
+    stores[1].start()
+    for cp in stores:
+        cp.wait()
 
     @pl.when(stays)
     def _():
@@ -288,13 +296,9 @@
 
     @pl.when(jnp.logical_not(stays))
     def _():
-        cp = copy(fin, igr, p2_s.at[0], p2_r.at[0], owner(z))
-        cp.start()
-        cp.wait()
+        home.wait()
         ig_out[...] = igr[...]
 
-    wcopy.wait_recv()
-    wg_out[other_rows, :] = wgr[...]
     for w in range(2):
         for t in range(nz):
             unless(jnp.logical_and(here, z == t), p_copy(w, t).wait_send)
@@ -345,7 +349,7 @@
         out_shape=(jax.ShapeDtypeStruct((feat, tok), BF16),
                    jax.ShapeDtypeStruct(first_weight.shape, BF16)),
         in_specs=[pl.BlockSpec(memory_space=pl.ANY)] * 4,
-        out_specs=(pl.BlockSpec(memory_space=pltpu.VMEM),) * 2,
+        out_specs=(pl.BlockSpec(memory_space=pltpu.VMEM), pl.BlockSpec(memory_space=pl.ANY)),
         scratch_shapes=scratch,
         compiler_params=pltpu.CompilerParams(
             collective_id=0, has_side_effects=True, vmem_limit_bytes=62 * 2 ** 20),

time: 97.3 us -> 97.1 us (level)
  no operation moved by 1% of the time
where the time goes in v5:
time: 97.1 us; the launch traced here: 96.9 us
  Pallas kernels  93.3 us (96%)
  local copies, waits for them, and re-layouts  2.94 us (3%)
    pallas_call x1, Pallas kernels, body(): pl.pallas_call(functools.partial(kernel, nz, scale), out_shape=(jax.Shape...  93.3 us
    unnamed x2, local copies, waits for them, and re-layouts  2.94 us

profile of v5, /device:TPU:49, one launch (start us, length us, event | category | flops | bytes accessed | tf_op | source)
XLA Modules:
  0.0 96.9 jit_solution(13489009531097996005)
XLA Ops:
  0.6 93.3 %block_backward.1 = (bf16[64,128]{1,0:T(8,128)(2,1)}, bf16[768,128]{1,0:T(8,128)(2,1)}) custom-call(bf16[64,128]{1,0:T(8,128)(2,1)} %bitcast.4, bf16[64,128]{1,0:T(8,128)(2,1)} %bitcast.5, bf16[768,128]{1,0:T(8,128)(2,1)} %w1.1, bf16[128,768]{1,0:T(8,128)(2,1)} %w2.1), custom_call_target="tpu_custom_call" | custom-call | tf_op jit(solution)/shard_map/block_backward/pallas_call | solution.py:347
  94.0 1.3 %copy.8 = bf16[128,64]{0,1:T(8,128)(2,1)} copy(bf16[128,64]{0,1:T(8,128)(2,1)} %bitcast.3) | data formatting | bytes 32768
  95.3 1.6 %copy.9 = bf16[768,128]{1,0:T(8,128)(2,1)} copy(bf16[768,128]{1,0:T(8,128)(2,1)} %get-tuple-element.9) | data formatting | bytes 393216
